TPU v7x, 256 devices: a whole 4x4x8 slice. The times are simulated.
256 devices in a mesh: row: 4 (over y), theta: 16 (over z, x_lo), axial: 4 (over x_hi, core).
Axes of the slice: x: 4 (x_hi: 2, x_lo: 2; x = x_hi * 2 + x_lo), y: 4, z: 8, core: 2. Of those that a mesh axis runs over, the one named last changes fastest.
Arguments:
- adjoint_state: float32 [4, 2, 5, 32, 512, 128], P('row', None, None, 'axial', 'theta'), may hold values from -6 to 6
- source: float32 [4, 2, 5, 32, 512, 128], P('row', None, None, 'axial', 'theta'), may hold values from -6 to 6
- time_step: float32 [4, 32, 512, 128], P('row', 'axial', 'theta'), may hold values from 0.05 to 0.25
- flux_jacobian: float32 [4, 3, 5, 5, 32, 128], P('row', None, None, None, 'axial'), may hold values from -2.5 to 2.5
- blade_count: int32 [4], P('row'), may hold values from 16 to 79
- mode_order: int32 [4, 512], P('row'), may hold values from 0 to 511, each once within a row
- giles_matrix: float32 [4, 2, 2, 2, 5, 5], P('row'), may hold values from -4.2 to 4.2
- coupling_matrix: float32 [4, 2, 2, 5, 5], P('row'), may hold values from -9 to 9
Outputs:
- new_state: float32 [4, 2, 5, 32, 512, 128], P('row', None, None, 'axial', 'theta')
Inputs may be any that keep to these rules, and one draw needn't show every extreme that they name: Each row of mode_order lists every number 0 to 511 once.
All inputs are finite; a program needn't handle non-finite values.
Results may differ from a plain program's by a relative error of at most 0.0001.
Values sent between devices are 32-bit elements; how exact they have to be, the bound alone decides.
A program may use at most 128 MiB of HBM per device.

v0:
```python
import functools
import math

import jax
import jax.numpy as jnp
from jax import lax
from jax.experimental import pallas as pl
from jax.experimental.pallas import tpu as pltpu
from jax.sharding import PartitionSpec as P

MESH = pl.DeviceIdType.MESH
F32 = jnp.float32
BF16 = jnp.bfloat16
MODES = 16
SECTIONS = 4
DISSIPATION = 0.05
OMEGA_UNIT = 0.02
LAYERS = 8
SECTOR = 32
RADII = 128
VARS = 5
PAD = 16
FIRST, LAST = PAD, PAD + SECTOR - 1
OWN = pl.ds(PAD, SECTOR)
BAND = 8
WIDE = 384
MODE_ROW = 100


def sin_cos(turns):
    h = (turns - jnp.floor(turns + 0.5)) * math.pi
    z = h * h
    s = 1.0 / 6227020800
    for d in (-39916800, 362880, -5040, 120, -6, 1):
        s = s * z + 1.0 / d
    s = s * h
    c = 1.0 / 479001600
    for d in (-3628800, 40320, -720, 24, -2, 1):
        c = c * z + 1.0 / d
    return 2.0 * s * c, 1.0 - 2.0 * s * s


def high(x):
    return x.astype(BF16).astype(F32)


def lanes(rows):
    return lax.broadcasted_iota(jnp.int32, (rows, 128), 1)


def subs(rows):
    return lax.broadcasted_iota(jnp.int32, (rows, 128), 0)


def wait_for(ref, sem):
    pltpu.make_async_copy(ref, ref, sem).wait()


def kernel(
    shape,
    state_in,
    source_in,
    step_in,
    jac_in,
    blade,
    order,
    giles,
    coupling,
    out,
    v,
    src,
    dt,
    jin,
    jb,
    t_out,
    t_in,
    wf,
    w2,
    e_tab,
    pack,
    parts,
    sent,
    got,
    dt_all,
    c_out,
    c_in,
    load_sem,
    th_send,
    th_recv,
    ax_send,
    ax_recv,
    dt_send,
    dt_recv,
    pk_sem,
    p_send,
    p_recv,
    c_send,
    c_recv,
    out_sem,
):
    nrow, nth, nax, circle = shape
    y, t, a = lax.axis_index("row"), lax.axis_index("theta"), lax.axis_index("axial")
    inlet, outlet = a == 0, a == nax - 1
    bnd = jnp.logical_or(inlet, outlet)
    inner = jnp.logical_not(bnd)
    side = jnp.where(inlet, 0, 1)
    paired = jnp.logical_or(
        jnp.logical_and(inlet, y > 0), jnp.logical_and(outlet, y < nrow - 1)
    )
    alone = jnp.logical_not(paired)
    py = jnp.where(paired, jnp.where(inlet, y - 1, y + 1), y)
    pa = jnp.where(paired, jnp.where(inlet, nax - 1, 0), a)
    edge = jnp.where(inlet, 1, LAYERS)

    def on_my_side(band):
        return jnp.logical_or(alone, lax.rem(band // 2, 2) == side)

    owner = jnp.logical_and(bnd, on_my_side(t))
    t_next, t_prev = lax.rem(t + 1, nth), lax.rem(t + nth - 1, nth)

    load_state = pltpu.make_async_copy(
        state_in.at[0], v.at[0, :, :, pl.ds(1, LAYERS), OWN], load_sem.at[0]
    )
    load_step = pltpu.make_async_copy(step_in.at[0], dt.at[:, OWN], load_sem.at[1])
    load_jac = pltpu.make_async_copy(jac_in.at[0], jin, load_sem.at[2])
    load_source = pltpu.make_async_copy(source_in.at[0], src, load_sem.at[3])
    load_state.start()
    load_step.start()
    load_jac.start()
    load_source.start()

    barrier = pltpu.get_barrier_semaphore()

    def hello(row, theta, axial):
        pl.semaphore_signal(
            barrier, inc=1, device_id=(row, theta, axial), device_id_type=MESH
        )

    hello(y, t_next, a)
    hello(y, t_prev, a)
    pl.when(a > 0)(lambda: hello(y, t, a - 1))
    pl.when(a < nax - 1)(lambda: hello(y, t, a + 1))

    @pl.when(bnd)
    def _():
        def greet(i, carry):
            other = lax.rem(t + i, nth)
            mine = on_my_side(other)

            @pl.when(jnp.logical_and(i > 0, jnp.logical_or(owner, mine)))
            def _():
                hello(y, other, a)

            @pl.when(
                jnp.logical_and(
                    paired, jnp.logical_or(owner, jnp.logical_not(mine))
                )
            )
            def _():
                hello(py, other, pa)

            return carry

        lax.fori_loop(0, nth, greet, 0)

    lane1, lane16, sub16 = lanes(1), lanes(16), subs(16)

    def mode_column(slot):
        row = pack[slot, pl.ds(MODE_ROW, 1), :]
        picked = jnp.where(lane16 == sub16, jnp.broadcast_to(row, (16, 128)), 0.0)
        return jnp.sum(picked, axis=1, keepdims=True)

    def full_table(slot):
        column = mode_column(slot)
        wide = lax.broadcasted_iota(jnp.int32, (16, circle), 1).astype(F32)
        sn, cs = sin_cos(wide * column * (1.0 / circle))
        table = jnp.concatenate(
            [
                jnp.concatenate([cs, sn], axis=1),
                jnp.concatenate([-sn, cs], axis=1),
            ],
            axis=0,
        )
        hi = table.astype(BF16)
        lo = (table - hi.astype(F32)).astype(BF16)
        e_tab[slot] = jnp.concatenate([hi, lo, hi, jnp.zeros_like(hi)], axis=0)

    @pl.when(bnd)
    def _():
        mrow = jnp.zeros((1, 128), F32)
        for k in range(MODES):
            m_k = order[0, k].astype(F32) - (circle // 2)
            mrow = jnp.where(lax.rem(lane1, MODES) == k, m_k, mrow)
        pack[0, pl.ds(MODE_ROW, 1), :] = mrow
        slope = mrow * (2.0 / circle)
        sign = jnp.where(lax.rem(lane1, 2 * MODES) < MODES, -1.0, 1.0)
        for c in range(VARS):
            for w in range(VARS):
                i = c * VARS + w
                pack[0, pl.ds(i, 1), :] = (
                    giles[0, side, 0, 0, c, w] + slope * giles[0, side, 1, 0, c, w]
                )
                pack[0, pl.ds(25 + i, 1), :] = sign * (
                    giles[0, side, 0, 1, c, w] + slope * giles[0, side, 1, 1, c, w]
                )
                pack[0, pl.ds(50 + i, 1), :] = jnp.broadcast_to(
                    coupling[0, side, 0, c, w], (1, 128)
                )
                pack[0, pl.ds(75 + i, 1), :] = sign * coupling[0, side, 1, c, w]
        first_cell = (t * SECTOR).astype(F32)
        cell = first_cell + lax.rem(lane16, SECTOR).astype(F32)
        sn, cs = sin_cos(cell * mode_column(0) * (1.0 / circle))
        real = lax.rem(lane16, 2 * SECTOR) < SECTOR
        table = jnp.concatenate(
            [jnp.where(real, cs, sn), jnp.where(real, -sn, cs)], axis=0
        ) * (1.0 / circle)
        hi = high(table)
        lo = jnp.where(lanes(32) < 64, table - hi, 0.0)
        wf[...] = jnp.concatenate([hi, lo], axis=1).astype(BF16)
        rows = SECTOR + 16
        cell = first_cell - 8.0 + subs(rows).astype(F32)
        sn, cs = sin_cos(cell * mrow * (1.0 / circle))
        real = lax.rem(lanes(rows), 2 * MODES) < MODES
        table = jnp.concatenate(
            [jnp.where(real, cs, -sn), jnp.where(real, sn, cs)], axis=0
        )
        hi = high(table)
        lane = lanes(2 * rows)
        w2[...] = jnp.where(
            lane < 64, hi, jnp.where(lane < 96, table - hi, 0.0)
        ).astype(BF16)
        parts[pl.ds(320, 64), :] = jnp.zeros((64, 128), F32)

    pl.when(owner)(lambda: full_table(0))

    @pl.when(inlet)
    def _():
        for q in range(SECTIONS):
            v[q, :, :, 0, :, :] = jnp.zeros((2, VARS, 2 * PAD + SECTOR, 128), F32)

    @pl.when(outlet)
    def _():
        for q in range(SECTIONS):
            v[q, :, :, LAYERS + 1, :, :] = jnp.zeros(
                (2, VARS, 2 * PAD + SECTOR, 128), F32
            )

    pl.semaphore_wait(
        barrier,
        2
        + jnp.where(a > 0, 1, 0)
        + jnp.where(a < nax - 1, 1, 0)
        + jnp.where(
            bnd,
            jnp.where(owner, jnp.where(paired, 2 * nth - 1, nth - 1), nth),
            0,
        ),
    )

    def remote(src_ref, dst_ref, send, recv, device):
        return pltpu.make_async_remote_copy(
            src_ref=src_ref,
            dst_ref=dst_ref,
            send_sem=send,
            recv_sem=recv,
            device_id=device,
            device_id_type=MESH,
        )

    def theta_copies(q):
        return [
            remote(
                t_out.at[q, i], t_in.at[q, 1 - i], th_send.at[q, i],
                th_recv.at[q, 1 - i], (y, (t_prev, t_next)[i], a),
            )
            for i in range(2)
        ]

    def send_theta(q):
        def stage(i, carry):
            for p in range(2):
                for c in range(VARS):
                    t_out[q, 0, p, c, pl.ds(i, 1), :] = v[q, p, c, i + 1, FIRST : FIRST + 1, :]
                    t_out[q, 1, p, c, pl.ds(i, 1), :] = v[q, p, c, i + 1, LAST : LAST + 1, :]
            return carry

        lax.fori_loop(0, LAYERS, stage, 0)
        for copy in theta_copies(q):
            copy.start()

    def take_theta(q):
        for copy in theta_copies(q):
            copy.wait_recv()

        def place(i, carry):
            for p in range(2):
                for c in range(VARS):
                    v[q, p, c, i + 1, FIRST - 1 : FIRST, :] = t_in[q, 0, p, c, pl.ds(i, 1), :]
                    v[q, p, c, i + 1, LAST + 1 : LAST + 2, :] = t_in[q, 1, p, c, pl.ds(i, 1), :]
            return carry

        lax.fori_loop(0, LAYERS, place, 0)

    def axial_down(q):
        return remote(
            v.at[q, :, :, 1, OWN], v.at[q, :, :, LAYERS + 1, OWN],
            ax_send.at[q, 0], ax_recv.at[q, 1], (y, t, a - 1),
        )

    def axial_up(q):
        return remote(
            v.at[q, :, :, LAYERS, OWN], v.at[q, :, :, 0, OWN],
            ax_send.at[q, 1], ax_recv.at[q, 0], (y, t, a + 1),
        )

    def send_axial(q):
        pl.when(a > 0)(lambda: axial_down(q).start())
        pl.when(a < nax - 1)(lambda: axial_up(q).start())

    def take_axial(q):
        pl.when(a > 0)(lambda: wait_for(v.at[q, :, :, 0, OWN], ax_recv.at[q, 0]))
        pl.when(a < nax - 1)(
            lambda: wait_for(v.at[q, :, :, LAYERS + 1, OWN], ax_recv.at[q, 1])
        )

    frequency = blade[0].astype(F32) * OMEGA_UNIT
    lane8 = lanes(8)

    def stencil(q, first, last):
        weight = 1.0 / (SECTIONS - q)

        def layer(l, carry):
            for half in range(2):
                bases = [PAD + 16 * half, PAD + 16 * half + 8]
                acc = {}

                def add(key, value):
                    acc[key] = acc[key] + value if key in acc else value

                for w in range(VARS):
                    deltas = {}
                    for ti, base in enumerate(bases):
                        for p in range(2):
                            mid = v[q, p, w, l, base : base + 8, :]
                            tp = v[q, p, w, l, base + 1 : base + 9, :]
                            tm = v[q, p, w, l, base - 1 : base + 7, :]
                            ap = v[q, p, w, l + 1, base : base + 8, :]
                            am = v[q, p, w, l - 1, base : base + 8, :]
                            rp = jnp.where(lane8 == 127, 0.0, pltpu.roll(mid, 127, 1))
                            rm = jnp.where(lane8 == 0, 0.0, pltpu.roll(mid, 1, 1))
                            deltas[0, p, ti] = ap - am
                            deltas[1, p, ti] = tp - tm
                            deltas[2, p, ti] = rp - rm
                            total = (ap + am) + (tp + tm) + (rp + rm)
                            add((p, w, ti), DISSIPATION * total - 6 * DISSIPATION * mid)
                            turn = frequency * mid
                            add((1 - p, w, ti), turn if p == 1 else -turn)
                    for d in range(3):
                        for c in range(VARS):
                            jac = jb[(d * VARS + w) * VARS + c, l - 1]
                            for ti in range(2):
                                for p in range(2):
                                    add((p, c, ti), jac * deltas[d, p, ti])
                for ti, base in enumerate(bases):
                    here = dt[l - 1, base : base + 8, :] * weight
                    for p in range(2):
                        for c in range(VARS):
                            forced = (
                                src[p, c, l - 1, base - PAD : base - PAD + 8, :]
                                + acc[p, c, ti]
                            )
                            v[q + 1, p, c, l, base : base + 8, :] = (
                                v[0, p, c, l, base : base + 8, :] + here * forced
                            )
            return carry

        lax.fori_loop(first, last, layer, 0)

    def forward(q, group):
        blocks = []
        for c in range(VARS):
            blocks.append(
                jnp.concatenate(
                    [v[q, p, c, edge, PAD : PAD + SECTOR, :] for p in range(2)], axis=0
                )
            )
        x = jnp.concatenate(blocks, axis=1)
        hi = x.astype(BF16)
        lo = (x - hi.astype(F32)).astype(BF16)
        rhs = jnp.concatenate([hi, lo, hi, jnp.zeros_like(hi)], axis=0)
        res = jnp.dot(wf[...], rhs, preferred_element_type=F32)
        for c in range(VARS):
            parts[pl.ds(32 * (group + c), 32), :] = res[:, 128 * c : 128 * (c + 1)]

    def send_parts(rd):
        for u in range(3):
            block = parts[pl.ds(128 * u, 128), :].T
            sent[rd, :, :, 128 * u : 128 * (u + 1)] = block.reshape(nth, BAND, 128)

        def one(i, carry):
            band = lax.rem(t + i, nth)
            mine = on_my_side(band)
            own = jnp.logical_and(mine, i == 0)

            @pl.when(own)
            def _():
                pltpu.make_async_copy(
                    sent.at[rd, band], got.at[rd, t], p_recv.at[rd, 0]
                ).start()

            @pl.when(jnp.logical_not(own))
            def _():
                remote(
                    sent.at[rd, band],
                    got.at[rd, jnp.where(mine, t, nth + t)],
                    p_send.at[rd],
                    p_recv.at[rd, jnp.where(mine, 0, 1)],
                    (jnp.where(mine, y, py), band, jnp.where(mine, a, pa)),
                ).start()

            return carry

        lax.fori_loop(0, nth, one, 0)

    def swapped(x):
        return jnp.where(lane8 < MODES, pltpu.roll(x, 128 - MODES, 1), pltpu.roll(x, MODES, 1))

    def mixed(slot, coeffs, neighbour):
        turned = [swapped(x) for x in coeffs]
        turned_n = [swapped(x) for x in neighbour]
        result = []
        for c in range(VARS):
            total = jnp.zeros((8, 128), F32)
            for w in range(VARS):
                i = c * VARS + w
                total = total + pack[slot, pl.ds(i, 1), :] * coeffs[w]
                total = total + pack[slot, pl.ds(25 + i, 1), :] * turned[w]
                total = total + pack[slot, pl.ds(50 + i, 1), :] * neighbour[w]
                total = total + pack[slot, pl.ds(75 + i, 1), :] * turned_n[w]
            result.append(jnp.where(lane8 < 2 * MODES, total, 0.0))
        return result

    def response(slot, coeffs):
        blocks = []
        for x in coeffs:
            hi = high(x)
            blocks.append(hi + pltpu.roll(hi, 32, 1) + pltpu.roll(x - hi, 64, 1))
        lhs = jnp.concatenate(blocks + [blocks[0]], axis=0).astype(BF16)
        fix = jnp.dot(lhs, e_tab[slot], preferred_element_type=F32)
        cells = dt_all[slot]
        cells = jnp.concatenate([cells, cells], axis=1)
        fix = fix * jnp.concatenate([cells] * (VARS + 1), axis=0)
        hi = fix.astype(BF16)
        lo = (fix - hi.astype(F32)).astype(BF16)
        res = lax.dot_general(
            jnp.concatenate([hi, lo], axis=0),
            e_tab[slot],
            (((1,), (1,)), ((), ())),
            preferred_element_type=F32,
        )
        half = BAND * (VARS + 1)
        result = []
        for c in range(VARS):
            top = res[BAND * c : BAND * (c + 1)]
            low = res[half + BAND * c : half + BAND * (c + 1)]
            result.append(top + pltpu.roll(top, 96, 1) + low)
        return result

    def serve(rd):
        q = 2 * rd
        wait_for(got.at[rd, pl.ds(0, nth)], p_recv.at[rd, 0])
        pl.when(paired)(
            lambda: wait_for(got.at[rd, pl.ds(nth, nth)], p_recv.at[rd, 1])
        )
        groups = []
        for slot in range(2):
            total = got[rd, slot * nth]
            for i in range(1, nth):
                total = total + got[rd, slot * nth + i]
            pieces = []
            for g in range(2 * VARS):
                piece = total[:, 128 * (g // 4) : 128 * (g // 4 + 1)]
                if g % 4:
                    piece = pltpu.roll(piece, 128 - 32 * (g % 4), 1)
                if slot == 1:
                    piece = jnp.where(paired, piece, 0.0)
                pieces.append(piece)
            groups.append((pieces[:VARS], pieces[VARS:]))
            if rd == 0:
                for u in range(nth // 4):
                    cells = jnp.zeros((8, 128), F32)
                    for i in range(4):
                        tile = got[rd, slot * nth + 4 * u + i, :, 256:384]
                        if i != 2:
                            tile = pltpu.roll(tile, (32 * i + 64) % 128, 1)
                        cells = jnp.where(lane8 // 32 == i, tile, cells)
                    dt_all[slot, :, 128 * u : 128 * (u + 1)] = cells
        (own_now, own_next), (nbr_now, nbr_next) = groups
        c_own = mixed(0, own_now, nbr_now)
        c_nbr = mixed(1, nbr_now, own_now)
        scale = 1.0 / (SECTIONS - q) / circle
        own_next = [x - scale * r for x, r in zip(own_next, response(0, c_own))]
        nbr_next = [
            jnp.where(paired, x - scale * r, 0.0)
            for x, r in zip(nbr_next, response(1, c_nbr))
        ]
        d_own = mixed(0, own_next, nbr_next)
        d_nbr = mixed(1, nbr_next, own_next)
        for slot, values in ((0, c_own + d_own), (1, c_nbr + d_nbr)):
            for u in range(3):
                total = jnp.zeros((8, 128), F32)
                for i, x in enumerate(values[4 * u : 4 * u + 4]):
                    total = total + (pltpu.roll(x, 32 * i, 1) if i else x)
                c_out[rd, slot, :, 128 * u : 128 * (u + 1)] = total

        def one(i, carry):
            theta = lax.rem(t + i, nth)

            @pl.when(i == 0)
            def _():
                pltpu.make_async_copy(
                    c_out.at[rd, 0], c_in.at[rd, t], c_recv.at[rd]
                ).start()

            @pl.when(i > 0)
            def _():
                remote(
                    c_out.at[rd, 0], c_in.at[rd, t], c_send.at[rd], c_recv.at[rd],
                    (y, theta, a),
                ).start()

            @pl.when(paired)
            def _():
                remote(
                    c_out.at[rd, 1], c_in.at[rd, t], c_send.at[rd], c_recv.at[rd],
                    (py, theta, pa),
                ).start()

            return carry

        lax.fori_loop(0, nth, one, 0)

    def fixes(rd):
        wait_for(c_in.at[rd], c_recv.at[rd])
        rows = []
        for u in range(3):
            block = c_in[rd, :, :, 128 * u : 128 * (u + 1)].reshape(RADII, 128).T
            rows.extend(block[32 * i : 32 * (i + 1)] for i in range(4))
        result = []
        for s in range(2):
            x = jnp.concatenate(rows[VARS * s : VARS * (s + 1)], axis=1)
            hi = x.astype(BF16)
            lo = (x - hi.astype(F32)).astype(BF16)
            rhs = jnp.concatenate([hi, lo, hi, jnp.zeros_like(hi)], axis=0)
            result.append(jnp.dot(w2[...], rhs, preferred_element_type=F32))
        return result

    def subtract(q, fix, margin):
        weight = 1.0 / (SECTIONS - q)
        rows = SECTOR + 2 * margin
        base = PAD - margin
        here = dt[edge - 1, base : base + rows, :] * weight
        for p in range(2):
            for c in range(VARS):
                top = 48 * p + 8 - margin
                v[q + 1, p, c, edge, base : base + rows, :] = (
                    v[q + 1, p, c, edge, base : base + rows, :]
                    - here * fix[top : top + rows, 128 * c : 128 * (c + 1)]
                )

    load_state.wait()
    send_theta(0)
    send_axial(0)
    load_step.wait()

    def dt_copies():
        return [
            remote(
                dt.at[edge - 1, pl.ds(PAD, 8)], dt.at[edge - 1, pl.ds(PAD + SECTOR, 8)],
                dt_send.at[0], dt_recv.at[0], (y, t_prev, a),
            ),
            remote(
                dt.at[edge - 1, pl.ds(PAD + SECTOR - 8, 8)], dt.at[edge - 1, pl.ds(PAD - 8, 8)],
                dt_send.at[1], dt_recv.at[1], (y, t_next, a),
            ),
        ]

    def pack_copy():
        return remote(pack.at[0], pack.at[1], pk_sem.at[0], pk_sem.at[1], (py, t, pa))

    helps = jnp.logical_and(bnd, jnp.logical_not(owner))
    served = jnp.logical_and(owner, paired)

    @pl.when(bnd)
    def _():
        for copy in dt_copies():
            copy.start()
        pl.when(helps)(lambda: pack_copy().start())
        parts[pl.ds(320, 32), :] = dt[edge - 1, PAD : PAD + SECTOR, :]
        forward(0, 0)

    load_jac.wait()

    def spread(l, carry):
        for d in range(3):
            for w in range(VARS):
                for c in range(VARS):
                    jb[(d * VARS + w) * VARS + c, l] = jnp.broadcast_to(
                        jin[d, w, c, pl.ds(l, 1), :] * 0.5, (8, 128)
                    )
        return carry

    lax.fori_loop(0, LAYERS, spread, 0)
    load_source.wait()

    rest = (jnp.where(inlet, 2, 1), jnp.where(outlet, LAYERS, LAYERS + 1))
    far = (jnp.where(inlet, 3, 1), jnp.where(outlet, LAYERS - 1, LAYERS + 1))
    near = jnp.where(inlet, 1, LAYERS - 1)

    def result_copy(start, count):
        return pltpu.make_async_copy(
            v.at[SECTIONS, :, :, pl.ds(start, count), OWN],
            out.at[0, :, :, pl.ds(start - 1, count)],
            out_sem,
        )

    for rd in range(2):
        q = 2 * rd
        take_theta(q)

        @pl.when(bnd)
        def _():
            stencil(q, edge, edge + 1)
            if rd:
                forward(q, 0)
            forward(q + 1, VARS)
            send_parts(rd)

        take_axial(q)
        stencil(q, *rest)
        send_theta(q + 1)
        send_axial(q + 1)

        if rd == 0:

            @pl.when(served)
            def _():
                pack_copy().wait_recv()
                full_table(1)

        pl.when(owner)(lambda: serve(rd))
        take_theta(q + 1)
        take_axial(q + 1)
        stencil(q + 1, *far)
        if rd == 0:
            send_axial(q + 2)
        else:
            pl.when(inner)(lambda: result_copy(1, LAYERS).start())
            pl.when(bnd)(lambda: result_copy(far[0], LAYERS - 2).start())

        @pl.when(bnd)
        def _():
            if rd == 0:
                for copy in dt_copies():
                    copy.wait_recv()
            now, later = fixes(rd)
            subtract(q, now, 8)
            stencil(q + 1, near, near + 2)
            subtract(q + 1, later, 0)
            if rd:
                result_copy(near, 2).start()

        if rd == 0:
            send_theta(q + 2)

    for q in range(SECTIONS):
        for copy in theta_copies(q):
            copy.wait_send()
        pl.when(a > 0)(lambda: axial_down(q).wait_send())
        pl.when(a < nax - 1)(lambda: axial_up(q).wait_send())

    @pl.when(bnd)
    def _():
        for copy in dt_copies():
            copy.wait_send()
        pl.when(helps)(lambda: pack_copy().wait_send())
        for rd in range(2):
            pl.when(owner)(
                lambda: wait_for(sent.at[rd, pl.ds(0, nth - 1)], p_send.at[rd])
            )
            pl.when(helps)(lambda: wait_for(sent.at[rd], p_send.at[rd]))
            pl.when(served)(
                lambda: wait_for(got.at[rd, pl.ds(0, 2 * nth - 1)], c_send.at[rd])
            )
            pl.when(jnp.logical_and(owner, alone))(
                lambda: wait_for(got.at[rd, pl.ds(0, nth - 1)], c_send.at[rd])
            )

    wait_for(v.at[SECTIONS, :, :, pl.ds(1, LAYERS), OWN], out_sem)


def solution(mesh):
    nrow, nth, nax = mesh.shape["row"], mesh.shape["theta"], mesh.shape["axial"]

    def step(state, source, time_step, jacobian, blade, order, giles, coupling):
        circle = order.shape[1]
        cells = (2, VARS)
        anyspace = pl.BlockSpec(memory_space=pl.ANY)
        scalars = pl.BlockSpec(memory_space=pltpu.SMEM)
        dma = pltpu.SemaphoreType.DMA
        return pl.pallas_call(
            functools.partial(kernel, (nrow, nth, nax, circle)),
            out_shape=jax.ShapeDtypeStruct(state.shape, F32),
            in_specs=[anyspace] * 4 + [scalars] * 4,
            out_specs=anyspace,
            scratch_shapes=[
                pltpu.VMEM((SECTIONS + 1, *cells, LAYERS + 2, 2 * PAD + SECTOR, RADII), F32),
                pltpu.VMEM((*cells, LAYERS, SECTOR, RADII), F32),
                pltpu.VMEM((LAYERS, 2 * PAD + SECTOR, RADII), F32),
                pltpu.VMEM((3, VARS, VARS, LAYERS, RADII), F32),
                pltpu.VMEM((75, LAYERS, 8, RADII), F32),
                pltpu.VMEM((SECTIONS, 2, *cells, LAYERS, RADII), F32),
                pltpu.VMEM((SECTIONS, 2, *cells, LAYERS, RADII), F32),
                pltpu.VMEM((32, 256), BF16),
                pltpu.VMEM((2 * (SECTOR + 16), 128), BF16),
                pltpu.VMEM((2, 128, 2 * circle), BF16),
                pltpu.VMEM((2, 104, 128), F32),
                pltpu.VMEM((WIDE, 128), F32),
                pltpu.VMEM((2, nth, BAND, WIDE), F32),
                pltpu.VMEM((2, 2 * nth, BAND, WIDE), F32),
                pltpu.VMEM((2, BAND, circle), F32),
                pltpu.VMEM((2, 2, BAND, WIDE), F32),
                pltpu.VMEM((2, nth, BAND, WIDE), F32),
                dma((4,)),
                dma((SECTIONS, 2)),
                dma((SECTIONS, 2)),
                dma((SECTIONS, 2)),
                dma((SECTIONS, 2)),
                dma((2,)),
                dma((2,)),
                dma((2,)),
                dma((2,)),
                dma((2, 2)),
                dma((2,)),
                dma((2,)),
                dma,
            ],
            compiler_params=pltpu.CompilerParams(
                collective_id=0, has_side_effects=True, vmem_limit_bytes=48 * 2**20
            ),
        )(state, source, time_step, jacobian, blade, order, giles, coupling)

    return jax.shard_map(
        step,
        mesh=mesh,
        in_specs=(
            P("row", None, None, "axial", "theta", None),
            P("row", None, None, "axial", "theta", None),
            P("row", "axial", "theta", None),
            P("row", None, None, None, "axial", None),
            P("row"),
            P("row", None),
            P("row", None, None, None, None, None),
            P("row", None, None, None, None),
        ),
        out_specs=P("row", None, None, "axial", "theta", None),
        check_vma=False,
    )
```

profile of v0, /device:TPU:7, one launch (start us, length us, event | category | flops | bytes accessed | tf_op | source)
XLA Modules:
  0.0 65.0 jit_solution(6880925631407044157)
XLA Ops:
  0.7 0.7 %copy.10.coupling = f32[1,2,2,5,5]{4,3,2,1,0:T(8,128)S(1)} copy(f32[1,2,2,5,5]{4,2,3,1,0:T(2,128)} %param.15) | data formatting | bytes 800 | tf_op args[7]
  1.4 0.7 %copy.9.giles = f32[1,2,2,2,5,5]{5,4,3,2,1,0:T(8,128)S(1)} copy(f32[1,2,2,2,5,5]{5,3,4,2,1,0:T(2,128)} %param.14) | data formatting | bytes 1600 | tf_op args[6]
  2.1 0.0 copy-start
  2.1 1.3 %copy-done = f32[1,2,5,8,32,128]{5,4,3,2,1,0:T(8,128)S(1)} copy-done((f32[1,2,5,8,32,128]{5,4,3,2,1,0:T(8,128)S(1)}, f32[1,2,5,8,32,128]{5,4,3,2,1,0:T(8,128)}, u32[]{:S(2)}) %copy-start) | copy-done | bytes 1310744
  3.4 0.0 copy-start.1
  3.4 1.3 %copy-done.1 = f32[1,2,5,8,32,128]{5,4,3,2,1,0:T(8,128)S(1)} copy-done((f32[1,2,5,8,32,128]{5,4,3,2,1,0:T(8,128)S(1)}, f32[1,2,5,8,32,128]{5,4,3,2,1,0:T(8,128)}, u32[]{:S(2)}) %copy-start.1) | copy-done | bytes 1310744
  4.7 0.0 copy-start.2
  4.7 1.0 %copy-done.2 = f32[1,3,5,5,8,128]{5,4,3,2,1,0:T(8,128)S(1)} copy-done((f32[1,3,5,5,8,128]{5,4,3,2,1,0:T(8,128)S(1)}, f32[1,3,5,5,8,128]{5,4,3,2,1,0:T(8,128)}, u32[]{:S(2)}) %copy-start.2) | copy-done | bytes 307224
  5.7 0.0 copy-start.3
  5.7 0.9 %copy-done.3 = f32[1,8,32,128]{3,2,1,0:T(8,128)S(1)} copy-done((f32[1,8,32,128]{3,2,1,0:T(8,128)S(1)}, f32[1,8,32,128]{3,2,1,0:T(8,128)}, u32[]{:S(2)}) %copy-start.3) | copy-done | bytes 131096
  6.6 0.0 copy-start.4
  6.6 0.7 %copy-done.4 = s32[1,512]{1,0:T(1,128)S(1)} copy-done((s32[1,512]{1,0:T(1,128)S(1)}, s32[1,512]{1,0:T(1,128)}, u32[]{:S(2)}) %copy-start.4) | copy-done | bytes 2072
  7.3 56.6 %shard_map.82 = f32[1,2,5,8,32,128]{5,4,3,2,1,0:T(8,128)S(1)} custom-call(f32[1,2,5,8,32,128]{5,4,3,2,1,0:T(8,128)S(1)} %copy-done, f32[1,2,5,8,32,128]{5,4,3,2,1,0:T(8,128)S(1)} %copy-done.1, f32[1,8,32,128]{3,2,1,0:T(8,128)S(1)} %copy-done.3, f32[1,3,5,5,8,128]{5,4,3,2,1,0:T(8,128)S(1)} %copy-done.2, s32[1]{0:T(128)S(6)} %copy.12.blade, ...), custom_call_target="tpu_custom_call" | custom-call | tf_op jit(solution)/shard_map/pallas_call | solution.py:711
  63.9 1.1 %copy.13 = f32[1,2,5,8,32,128]{5,4,3,2,1,0:T(8,128)} copy(f32[1,2,5,8,32,128]{5,4,3,2,1,0:T(8,128)S(1)} %shard_map.82) | data formatting | bytes 2621440
Async XLA Ops:
  2.1 1.3 %copy-start = (f32[1,2,5,8,32,128]{5,4,3,2,1,0:T(8,128)S(1)}, f32[1,2,5,8,32,128]{5,4,3,2,1,0:T(8,128)}, u32[]{:S(2)}) copy-start(f32[1,2,5,8,32,128]{5,4,3,2,1,0:T(8,128)} %state_in.1) | copy-start | bytes 3932164
  3.4 1.3 %copy-start.1 = (f32[1,2,5,8,32,128]{5,4,3,2,1,0:T(8,128)S(1)}, f32[1,2,5,8,32,128]{5,4,3,2,1,0:T(8,128)}, u32[]{:S(2)}) copy-start(f32[1,2,5,8,32,128]{5,4,3,2,1,0:T(8,128)} %source_in.1) | copy-start | bytes 3932164
  4.7 1.0 %copy-start.2 = (f32[1,3,5,5,8,128]{5,4,3,2,1,0:T(8,128)S(1)}, f32[1,3,5,5,8,128]{5,4,3,2,1,0:T(8,128)}, u32[]{:S(2)}) copy-start(f32[1,3,5,5,8,128]{5,4,3,2,1,0:T(8,128)} %jac_in.1) | copy-start | bytes 921604
  5.7 0.9 %copy-start.3 = (f32[1,8,32,128]{3,2,1,0:T(8,128)S(1)}, f32[1,8,32,128]{3,2,1,0:T(8,128)}, u32[]{:S(2)}) copy-start(f32[1,8,32,128]{3,2,1,0:T(8,128)} %step_in.1) | copy-start | bytes 393220
  6.6 0.7 %copy-start.4 = (s32[1,512]{1,0:T(1,128)S(1)}, s32[1,512]{1,0:T(1,128)}, u32[]{:S(2)}) copy-start(s32[1,512]{1,0:T(1,128)} %order.1) | copy-start | bytes 6148
where the time goes:
time: 65.3 us; the launch traced here: 65 us
  Pallas kernels  56.6 us (87%)
  local copies, waits for them, and re-layouts  7.68 us (12%)
  between operations  0.67 us (1%)
    pallas_call x1, Pallas kernels, step(): pl.pallas_call(functools.partial(kernel, (nrow, nth, nax, circle)), out_s...  56.6 us
    unnamed x13, local copies, waits for them, and re-layouts  7.68 us

commit v1 on v0

--- a/solution.py
+++ b/solution.py
@@ -25,6 +25,7 @@
 BAND = 8
 WIDE = 384
 MODE_ROW = 100
+VMEM_LIMIT = 48 * 2**20
 
 
 def sin_cos(turns):
@@ -62,13 +63,14 @@
     source_in,
     step_in,
     jac_in,
-    blade,
     order,
     giles,
     coupling,
+    blade,
     out,
     v,
     src,
+    src_edge,
     dt,
     jin,
     jb,
@@ -89,20 +91,20 @@
     th_recv,
     ax_send,
     ax_recv,
-    dt_send,
-    dt_recv,
+    edge_send,
+    edge_recv,
+    tile_send,
+    tile_recv,
     pk_sem,
     p_send,
     p_recv,
     c_send,
     c_recv,
-    out_sem,
 ):
     nrow, nth, nax, circle = shape
     y, t, a = lax.axis_index("row"), lax.axis_index("theta"), lax.axis_index("axial")
     inlet, outlet = a == 0, a == nax - 1
     bnd = jnp.logical_or(inlet, outlet)
-    inner = jnp.logical_not(bnd)
     side = jnp.where(inlet, 0, 1)
     paired = jnp.logical_or(
         jnp.logical_and(inlet, y > 0), jnp.logical_and(outlet, y < nrow - 1)
@@ -116,6 +118,14 @@
         return jnp.logical_or(alone, lax.rem(band // 2, 2) == side)
 
     owner = jnp.logical_and(bnd, on_my_side(t))
+    nz = nth // 2
+
+    def far_first(i):
+        step = i // 2
+        away = (step + 1) // 2
+        dz = nz // 2 + jnp.where(lax.rem(step, 2) == 0, away, -away)
+        return 2 * lax.rem(t // 2 + dz, nz) + lax.rem(i, 2)
+
     t_next, t_prev = lax.rem(t + 1, nth), lax.rem(t + nth - 1, nth)
 
     load_state = pltpu.make_async_copy(
@@ -144,10 +154,10 @@
     @pl.when(bnd)
     def _():
         def greet(i, carry):
-            other = lax.rem(t + i, nth)
+            other = far_first(i)
             mine = on_my_side(other)
 
-            @pl.when(jnp.logical_and(i > 0, jnp.logical_or(owner, mine)))
+            @pl.when(jnp.logical_and(other != t, jnp.logical_or(owner, mine)))
             def _():
                 hello(y, other, a)
 
@@ -198,15 +208,15 @@
             for w in range(VARS):
                 i = c * VARS + w
                 pack[0, pl.ds(i, 1), :] = (
-                    giles[0, side, 0, 0, c, w] + slope * giles[0, side, 1, 0, c, w]
+                    giles[0, side, 0, c, 0, w] + slope * giles[0, side, 1, c, 0, w]
                 )
                 pack[0, pl.ds(25 + i, 1), :] = sign * (
-                    giles[0, side, 0, 1, c, w] + slope * giles[0, side, 1, 1, c, w]
+                    giles[0, side, 0, c, 1, w] + slope * giles[0, side, 1, c, 1, w]
                 )
                 pack[0, pl.ds(50 + i, 1), :] = jnp.broadcast_to(
-                    coupling[0, side, 0, c, w], (1, 128)
+                    coupling[0, side, c, 0, w], (1, 128)
                 )
-                pack[0, pl.ds(75 + i, 1), :] = sign * coupling[0, side, 1, c, w]
+                pack[0, pl.ds(75 + i, 1), :] = sign * coupling[0, side, c, 1, w]
         first_cell = (t * SECTOR).astype(F32)
         cell = first_cell + lax.rem(lane16, SECTOR).astype(F32)
         sn, cs = sin_cos(cell * mode_column(0) * (1.0 / circle))
@@ -257,6 +267,8 @@
         ),
     )
 
+    rest = (jnp.where(inlet, 2, 1), jnp.where(outlet, LAYERS, LAYERS + 1))
+
     def remote(src_ref, dst_ref, send, recv, device):
         return pltpu.make_async_remote_copy(
             src_ref=src_ref,
@@ -299,7 +311,10 @@
                     v[q, p, c, i + 1, LAST + 1 : LAST + 2, :] = t_in[q, 1, p, c, pl.ds(i, 1), :]
             return carry
 
-        lax.fori_loop(0, LAYERS, place, 0)
+        if q < SECTIONS - 1:
+            lax.fori_loop(rest[0] - 1, rest[1] - 1, place, 0)
+        else:
+            lax.fori_loop(0, LAYERS, place, 0)
 
     def axial_down(q):
         return remote(
@@ -326,52 +341,63 @@
     frequency = blade[0].astype(F32) * OMEGA_UNIT
     lane8 = lanes(8)
 
+    def forcing(p, c, l, base):
+        if base < PAD:
+            return src_edge[0, p, c]
+        if base >= PAD + SECTOR:
+            return src_edge[1, p, c]
+        return src[p, c, l - 1, base - PAD : base - PAD + 8, :]
+
+    def tile_pair(q, l, first_row):
+        weight = 1.0 / (SECTIONS - q)
+        bases = [first_row, first_row + 8]
+        acc = {}
+
+        def add(key, value):
+            acc[key] = acc[key] + value if key in acc else value
+
+        for w in range(VARS):
+            deltas = {}
+            for ti, base in enumerate(bases):
+                for p in range(2):
+                    mid = v[q, p, w, l, base : base + 8, :]
+                    tp = v[q, p, w, l, base + 1 : base + 9, :]
+                    tm = v[q, p, w, l, base - 1 : base + 7, :]
+                    ap = v[q, p, w, l + 1, base : base + 8, :]
+                    am = v[q, p, w, l - 1, base : base + 8, :]
+                    rp = jnp.where(lane8 == 127, 0.0, pltpu.roll(mid, 127, 1))
+                    rm = jnp.where(lane8 == 0, 0.0, pltpu.roll(mid, 1, 1))
+                    deltas[0, p, ti] = ap - am
+                    deltas[1, p, ti] = tp - tm
+                    deltas[2, p, ti] = rp - rm
+                    total = (ap + am) + (tp + tm) + (rp + rm)
+                    add((p, w, ti), DISSIPATION * total - 6 * DISSIPATION * mid)
+                    turn = frequency * mid
+                    add((1 - p, w, ti), turn if p == 1 else -turn)
+            for d in range(3):
+                for c in range(VARS):
+                    jac = jb[(d * VARS + w) * VARS + c, l - 1]
+                    for ti in range(2):
+                        for p in range(2):
+                            add((p, c, ti), jac * deltas[d, p, ti])
+        for ti, base in enumerate(bases):
+            here = dt[l - 1, base : base + 8, :] * weight
+            for p in range(2):
+                for c in range(VARS):
+                    forced = (
+                        forcing(p, c, l, base)
+                        + acc[p, c, ti]
+                    )
+                    value = v[0, p, c, l, base : base + 8, :] + here * forced
+                    if q == SECTIONS - 1:
+                        out[0, p, c, l - 1, base - PAD : base - PAD + 8, :] = value
+                    else:
+                        v[q + 1, p, c, l, base : base + 8, :] = value
+
     def stencil(q, first, last):
-        weight = 1.0 / (SECTIONS - q)
-
         def layer(l, carry):
             for half in range(2):
-                bases = [PAD + 16 * half, PAD + 16 * half + 8]
-                acc = {}
-
-                def add(key, value):
-                    acc[key] = acc[key] + value if key in acc else value
-
-                for w in range(VARS):
-                    deltas = {}
-                    for ti, base in enumerate(bases):
-                        for p in range(2):
-                            mid = v[q, p, w, l, base : base + 8, :]
-                            tp = v[q, p, w, l, base + 1 : base + 9, :]
-                            tm = v[q, p, w, l, base - 1 : base + 7, :]
-                            ap = v[q, p, w, l + 1, base : base + 8, :]
-                            am = v[q, p, w, l - 1, base : base + 8, :]
-                            rp = jnp.where(lane8 == 127, 0.0, pltpu.roll(mid, 127, 1))
-                            rm = jnp.where(lane8 == 0, 0.0, pltpu.roll(mid, 1, 1))
-                            deltas[0, p, ti] = ap - am
-                            deltas[1, p, ti] = tp - tm
-                            deltas[2, p, ti] = rp - rm
-                            total = (ap + am) + (tp + tm) + (rp + rm)
-                            add((p, w, ti), DISSIPATION * total - 6 * DISSIPATION * mid)
-                            turn = frequency * mid
-                            add((1 - p, w, ti), turn if p == 1 else -turn)
-                    for d in range(3):
-                        for c in range(VARS):
-                            jac = jb[(d * VARS + w) * VARS + c, l - 1]
-                            for ti in range(2):
-                                for p in range(2):
-                                    add((p, c, ti), jac * deltas[d, p, ti])
-                for ti, base in enumerate(bases):
-                    here = dt[l - 1, base : base + 8, :] * weight
-                    for p in range(2):
-                        for c in range(VARS):
-                            forced = (
-                                src[p, c, l - 1, base - PAD : base - PAD + 8, :]
-                                + acc[p, c, ti]
-                            )
-                            v[q + 1, p, c, l, base : base + 8, :] = (
-                                v[0, p, c, l, base : base + 8, :] + here * forced
-                            )
+                tile_pair(q, l, PAD + 16 * half)
             return carry
 
         lax.fori_loop(first, last, layer, 0)
@@ -398,9 +424,9 @@
             sent[rd, :, :, 128 * u : 128 * (u + 1)] = block.reshape(nth, BAND, 128)
 
         def one(i, carry):
-            band = lax.rem(t + i, nth)
+            band = far_first(i)
             mine = on_my_side(band)
-            own = jnp.logical_and(mine, i == 0)
+            own = jnp.logical_and(mine, band == t)
 
             @pl.when(own)
             def _():
@@ -514,26 +540,26 @@
                 c_out[rd, slot, :, 128 * u : 128 * (u + 1)] = total
 
         def one(i, carry):
-            theta = lax.rem(t + i, nth)
-
-            @pl.when(i == 0)
+            theta = far_first(i)
+
+            @pl.when(paired)
             def _():
-                pltpu.make_async_copy(
-                    c_out.at[rd, 0], c_in.at[rd, t], c_recv.at[rd]
+                remote(
+                    c_out.at[rd, 1], c_in.at[rd, t], c_send.at[rd], c_recv.at[rd],
+                    (py, theta, pa),
                 ).start()
 
-            @pl.when(i > 0)
+            @pl.when(theta != t)
             def _():
                 remote(
                     c_out.at[rd, 0], c_in.at[rd, t], c_send.at[rd], c_recv.at[rd],
                     (y, theta, a),
                 ).start()
 
-            @pl.when(paired)
+            @pl.when(theta == t)
             def _():
-                remote(
-                    c_out.at[rd, 1], c_in.at[rd, t], c_send.at[rd], c_recv.at[rd],
-                    (py, theta, pa),
+                pltpu.make_async_copy(
+                    c_out.at[rd, 0], c_in.at[rd, t], c_recv.at[rd]
                 ).start()
 
             return carry
@@ -563,39 +589,67 @@
         for p in range(2):
             for c in range(VARS):
                 top = 48 * p + 8 - margin
-                v[q + 1, p, c, edge, base : base + rows, :] = (
-                    v[q + 1, p, c, edge, base : base + rows, :]
-                    - here * fix[top : top + rows, 128 * c : 128 * (c + 1)]
-                )
+                less = here * fix[top : top + rows, 128 * c : 128 * (c + 1)]
+                if q == SECTIONS - 1:
+                    out[0, p, c, edge - 1] = out[0, p, c, edge - 1] - less
+                else:
+                    v[q + 1, p, c, edge, base : base + rows, :] = (
+                        v[q + 1, p, c, edge, base : base + rows, :] - less
+                    )
+
+    def edge_copies():
+        plane = edge - 1
+        copies = []
+        for i, (at_, row, device) in enumerate(
+            ((0, PAD + SECTOR, t_prev), (SECTOR - 8, PAD - 8, t_next))
+        ):
+            rows, place, device = pl.ds(at_, 8), pl.ds(row, 8), (y, device, a)
+            copies += [
+                remote(
+                    state_in.at[0, :, :, plane, rows], v.at[0, :, :, edge, place],
+                    edge_send.at[0, i], edge_recv.at[0, i], device,
+                ),
+                remote(
+                    step_in.at[0, plane, rows], dt.at[plane, place],
+                    edge_send.at[1, i], edge_recv.at[1, i], device,
+                ),
+                remote(
+                    source_in.at[0, :, :, plane, rows], src_edge.at[1 - i],
+                    edge_send.at[2, i], edge_recv.at[2, i], device,
+                ),
+            ]
+        return copies
+
+    def tile_copies():
+        return [
+            remote(
+                v.at[1, :, :, edge, pl.ds(at_, 8)], v.at[1, :, :, edge, pl.ds(row, 8)],
+                tile_send.at[i], tile_recv.at[i], (y, device, a),
+            )
+            for i, (at_, row, device) in enumerate(
+                ((PAD, PAD + SECTOR, t_prev), (PAD + SECTOR - 8, PAD - 8, t_next))
+            )
+        ]
+
+    def pack_copy():
+        return remote(pack.at[0], pack.at[1], pk_sem.at[0], pk_sem.at[1], (py, t, pa))
+
+    helps = jnp.logical_and(bnd, jnp.logical_not(owner))
+    served = jnp.logical_and(owner, paired)
+
+    @pl.when(bnd)
+    def _():
+        for copy in edge_copies():
+            copy.start()
+        pl.when(helps)(lambda: pack_copy().start())
 
     load_state.wait()
     send_theta(0)
     send_axial(0)
     load_step.wait()
 
-    def dt_copies():
-        return [
-            remote(
-                dt.at[edge - 1, pl.ds(PAD, 8)], dt.at[edge - 1, pl.ds(PAD + SECTOR, 8)],
-                dt_send.at[0], dt_recv.at[0], (y, t_prev, a),
-            ),
-            remote(
-                dt.at[edge - 1, pl.ds(PAD + SECTOR - 8, 8)], dt.at[edge - 1, pl.ds(PAD - 8, 8)],
-                dt_send.at[1], dt_recv.at[1], (y, t_next, a),
-            ),
-        ]
-
-    def pack_copy():
-        return remote(pack.at[0], pack.at[1], pk_sem.at[0], pk_sem.at[1], (py, t, pa))
-
-    helps = jnp.logical_and(bnd, jnp.logical_not(owner))
-    served = jnp.logical_and(owner, paired)
-
     @pl.when(bnd)
     def _():
-        for copy in dt_copies():
-            copy.start()
-        pl.when(helps)(lambda: pack_copy().start())
         parts[pl.ds(320, 32), :] = dt[edge - 1, PAD : PAD + SECTOR, :]
         forward(0, 0)
 
@@ -613,29 +667,29 @@
     lax.fori_loop(0, LAYERS, spread, 0)
     load_source.wait()
 
-    rest = (jnp.where(inlet, 2, 1), jnp.where(outlet, LAYERS, LAYERS + 1))
     far = (jnp.where(inlet, 3, 1), jnp.where(outlet, LAYERS - 1, LAYERS + 1))
     near = jnp.where(inlet, 1, LAYERS - 1)
-
-    def result_copy(start, count):
-        return pltpu.make_async_copy(
-            v.at[SECTIONS, :, :, pl.ds(start, count), OWN],
-            out.at[0, :, :, pl.ds(start - 1, count)],
-            out_sem,
-        )
+    second = jnp.where(inlet, 2, LAYERS - 1)
 
     for rd in range(2):
         q = 2 * rd
-        take_theta(q)
 
         @pl.when(bnd)
         def _():
-            stencil(q, edge, edge + 1)
+            if rd == 0:
+                for copy in edge_copies():
+                    copy.wait_recv()
+            for half in range(2):
+                tile_pair(q, edge, PAD + 16 * half)
             if rd:
                 forward(q, 0)
             forward(q + 1, VARS)
             send_parts(rd)
-
+            if rd == 0:
+                for copy in tile_copies():
+                    copy.start()
+
+        take_theta(q)
         take_axial(q)
         stencil(q, *rest)
         send_theta(q + 1)
@@ -654,21 +708,22 @@
         stencil(q + 1, *far)
         if rd == 0:
             send_axial(q + 2)
-        else:
-            pl.when(inner)(lambda: result_copy(1, LAYERS).start())
-            pl.when(bnd)(lambda: result_copy(far[0], LAYERS - 2).start())
 
         @pl.when(bnd)
         def _():
+            now, later = fixes(rd)
             if rd == 0:
-                for copy in dt_copies():
-                    copy.wait_recv()
-            now, later = fixes(rd)
-            subtract(q, now, 8)
-            stencil(q + 1, near, near + 2)
-            subtract(q + 1, later, 0)
-            if rd:
-                result_copy(near, 2).start()
+                for copy in tile_copies():
+                    copy.wait()
+                subtract(q, now, 8)
+                for third in range(3):
+                    tile_pair(q + 1, edge, PAD - 8 + 16 * third)
+                stencil(q + 1, second, second + 1)
+                subtract(q + 1, later, 8)
+            else:
+                subtract(q, now, 8)
+                stencil(q + 1, near, near + 2)
+                subtract(q + 1, later, 0)
 
         if rd == 0:
             send_theta(q + 2)
@@ -681,7 +736,7 @@
 
     @pl.when(bnd)
     def _():
-        for copy in dt_copies():
+        for copy in edge_copies():
             copy.wait_send()
         pl.when(helps)(lambda: pack_copy().wait_send())
         for rd in range(2):
@@ -696,26 +751,27 @@
                 lambda: wait_for(got.at[rd, pl.ds(0, nth - 1)], c_send.at[rd])
             )
 
-    wait_for(v.at[SECTIONS, :, :, pl.ds(1, LAYERS), OWN], out_sem)
-
 
 def solution(mesh):
     nrow, nth, nax = mesh.shape["row"], mesh.shape["theta"], mesh.shape["axial"]
 
     def step(state, source, time_step, jacobian, blade, order, giles, coupling):
         circle = order.shape[1]
+        giles = giles.transpose(0, 1, 2, 4, 3, 5)
+        coupling = coupling.transpose(0, 1, 3, 2, 4)
         cells = (2, VARS)
         anyspace = pl.BlockSpec(memory_space=pl.ANY)
         scalars = pl.BlockSpec(memory_space=pltpu.SMEM)
         dma = pltpu.SemaphoreType.DMA
         return pl.pallas_call(
             functools.partial(kernel, (nrow, nth, nax, circle)),
-            out_shape=jax.ShapeDtypeStruct(state.shape, F32),
+            out_shape=pltpu.VMEM(state.shape, F32),
             in_specs=[anyspace] * 4 + [scalars] * 4,
-            out_specs=anyspace,
+            out_specs=pl.BlockSpec(memory_space=pltpu.VMEM),
             scratch_shapes=[
-                pltpu.VMEM((SECTIONS + 1, *cells, LAYERS + 2, 2 * PAD + SECTOR, RADII), F32),
+                pltpu.VMEM((SECTIONS, *cells, LAYERS + 2, 2 * PAD + SECTOR, RADII), F32),
                 pltpu.VMEM((*cells, LAYERS, SECTOR, RADII), F32),
+                pltpu.VMEM((2, *cells, 8, RADII), F32),
                 pltpu.VMEM((LAYERS, 2 * PAD + SECTOR, RADII), F32),
                 pltpu.VMEM((3, VARS, VARS, LAYERS, RADII), F32),
                 pltpu.VMEM((75, LAYERS, 8, RADII), F32),
@@ -736,6 +792,8 @@
                 dma((SECTIONS, 2)),
                 dma((SECTIONS, 2)),
                 dma((SECTIONS, 2)),
+                dma((3, 2)),
+                dma((3, 2)),
                 dma((2,)),
                 dma((2,)),
                 dma((2,)),
@@ -743,12 +801,17 @@
                 dma((2, 2)),
                 dma((2,)),
                 dma((2,)),
-                dma,
             ],
             compiler_params=pltpu.CompilerParams(
-                collective_id=0, has_side_effects=True, vmem_limit_bytes=48 * 2**20
+                collective_id=0, has_side_effects=True, vmem_limit_bytes=VMEM_LIMIT
             ),
-        )(state, source, time_step, jacobian, blade, order, giles, coupling)
+        )(
+            *(
+                pltpu.with_memory_space_constraint(x, pltpu.HBM)
+                for x in (state, source, time_step, jacobian, order, giles, coupling)
+            ),
+            blade,
+        )
 
     return jax.shard_map(
         step,

time: 65.3 us -> 51.5 us (0.79)
  Pallas kernels: 56.6 us -> 49.6 us
  local copies, waits for them, and re-layouts: 7.68 us -> 1.06 us
    pallas_call x1, Pallas kernels: 56.6 us -> 49.6 us  [step(): pl.pallas_call(functools.partial(kernel, (nrow, nth, nax, circle)), out_s...]
    unnamed x13 -> x1, local copies, waits for them, and re-layouts: 7.68 us -> 1.06 us
where the time goes in v1:
time: 51.5 us; the launch traced here: 51.3 us
  Pallas kernels  49.6 us (96%)
  local copies, waits for them, and re-layouts  1.06 us (2%)
  between operations  0.66 us (1%)
    pallas_call x1, Pallas kernels, step(): pl.pallas_call(functools.partial(kernel, (nrow, nth, nax, circle)), out_s...  49.6 us
    unnamed x1, local copies, waits for them, and re-layouts  1.06 us

profile of v1, /device:TPU:7, one launch (start us, length us, event | category | flops | bytes accessed | tf_op | source)
XLA Modules:
  0.0 51.3 jit_solution(18245621409724832819)
XLA Ops:
  0.7 49.6 %shard_map.82 = f32[1,2,5,8,32,128]{5,4,3,2,1,0:T(8,128)S(1)} custom-call(f32[1,2,5,8,32,128]{5,4,3,2,1,0:T(8,128)} %state_in.1, f32[1,2,5,8,32,128]{5,4,3,2,1,0:T(8,128)} %source_in.1, f32[1,8,32,128]{3,2,1,0:T(8,128)} %step_in.1, f32[1,3,5,5,8,128]{5,4,3,2,1,0:T(8,128)} %jac_in.1, s32[1,512]{1,0:T(1,128)} %order.1, f32[1,2,2,5,2,5]{5,4,3,2,1,0:T(2,128)} %bitcast.2, ...), custom_call_target="tpu_custom_call" | custom-call | tf_op jit(solution)/shard_map/pallas_call | solution.py:766
  50.3 1.1 %copy.10 = f32[1,2,5,8,32,128]{5,4,3,2,1,0:T(8,128)} copy(f32[1,2,5,8,32,128]{5,4,3,2,1,0:T(8,128)S(1)} %shard_map.82) | data formatting | bytes 2621440

commit v2 on v1

--- a/solution.py
+++ b/solution.py
@@ -23,7 +23,6 @@
 FIRST, LAST = PAD, PAD + SECTOR - 1
 OWN = pl.ds(PAD, SECTOR)
 BAND = 8
-WIDE = 384
 MODE_ROW = 100
 VMEM_LIMIT = 48 * 2**20
 
@@ -63,11 +62,14 @@
     source_in,
     step_in,
     jac_in,
+    order_in,
+    giles_in,
+    coupling_in,
+    blade,
+    out,
     order,
     giles,
     coupling,
-    blade,
-    out,
     v,
     src,
     src_edge,
@@ -82,10 +84,16 @@
     pack,
     parts,
     sent,
+    sent_x,
     got,
+    got_x,
+    got_dt,
     dt_all,
     c_out,
+    c_out_x,
     c_in,
+    c_in_x,
+    spare,
     load_sem,
     th_send,
     th_recv,
@@ -98,8 +106,12 @@
     pk_sem,
     p_send,
     p_recv,
+    x_send,
+    x_recv,
     c_send,
     c_recv,
+    y_send,
+    y_recv,
 ):
     nrow, nth, nax, circle = shape
     y, t, a = lax.axis_index("row"), lax.axis_index("theta"), lax.axis_index("axial")
@@ -134,10 +146,12 @@
     load_step = pltpu.make_async_copy(step_in.at[0], dt.at[:, OWN], load_sem.at[1])
     load_jac = pltpu.make_async_copy(jac_in.at[0], jin, load_sem.at[2])
     load_source = pltpu.make_async_copy(source_in.at[0], src, load_sem.at[3])
+    load_small = [
+        pltpu.make_async_copy(order_in, order, load_sem.at[4]),
+        pltpu.make_async_copy(giles_in, giles, load_sem.at[5]),
+        pltpu.make_async_copy(coupling_in, coupling, load_sem.at[6]),
+    ]
     load_state.start()
-    load_step.start()
-    load_jac.start()
-    load_source.start()
 
     barrier = pltpu.get_barrier_semaphore()
 
@@ -172,6 +186,16 @@
             return carry
 
         lax.fori_loop(0, nth, greet, 0)
+
+    load_step.start()
+
+    @pl.when(bnd)
+    def _():
+        for copy in load_small:
+            copy.start()
+
+    load_jac.start()
+    load_source.start()
 
     lane1, lane16, sub16 = lanes(1), lanes(16), subs(16)
 
@@ -197,6 +221,8 @@
 
     @pl.when(bnd)
     def _():
+        for copy in load_small:
+            copy.wait()
         mrow = jnp.zeros((1, 128), F32)
         for k in range(MODES):
             m_k = order[0, k].astype(F32) - (circle // 2)
@@ -239,7 +265,7 @@
         w2[...] = jnp.where(
             lane < 64, hi, jnp.where(lane < 96, table - hi, 0.0)
         ).astype(BF16)
-        parts[pl.ds(320, 64), :] = jnp.zeros((64, 128), F32)
+        parts[pl.ds(160, 96), :] = jnp.zeros((96, 128), F32)
 
     pl.when(owner)(lambda: full_table(0))
 
@@ -267,8 +293,6 @@
         ),
     )
 
-    rest = (jnp.where(inlet, 2, 1), jnp.where(outlet, LAYERS, LAYERS + 1))
-
     def remote(src_ref, dst_ref, send, recv, device):
         return pltpu.make_async_remote_copy(
             src_ref=src_ref,
@@ -288,15 +312,18 @@
             for i in range(2)
         ]
 
+    def flat(q, p, c):
+        return v.at[q, p, c].reshape((LAYERS + 2) * (2 * PAD + SECTOR), RADII)
+
+    def column(row):
+        return pl.ds(2 * PAD + SECTOR + row, LAYERS, stride=2 * PAD + SECTOR)
+
     def send_theta(q):
-        def stage(i, carry):
-            for p in range(2):
-                for c in range(VARS):
-                    t_out[q, 0, p, c, pl.ds(i, 1), :] = v[q, p, c, i + 1, FIRST : FIRST + 1, :]
-                    t_out[q, 1, p, c, pl.ds(i, 1), :] = v[q, p, c, i + 1, LAST : LAST + 1, :]
-            return carry
-
-        lax.fori_loop(0, LAYERS, stage, 0)
+        for p in range(2):
+            for c in range(VARS):
+                rows = flat(q, p, c)
+                t_out[q, 0, p, c] = rows[column(FIRST), :]
+                t_out[q, 1, p, c] = rows[column(LAST), :]
         for copy in theta_copies(q):
             copy.start()
 
@@ -304,17 +331,11 @@
         for copy in theta_copies(q):
             copy.wait_recv()
 
-        def place(i, carry):
-            for p in range(2):
-                for c in range(VARS):
-                    v[q, p, c, i + 1, FIRST - 1 : FIRST, :] = t_in[q, 0, p, c, pl.ds(i, 1), :]
-                    v[q, p, c, i + 1, LAST + 1 : LAST + 2, :] = t_in[q, 1, p, c, pl.ds(i, 1), :]
-            return carry
-
-        if q < SECTIONS - 1:
-            lax.fori_loop(rest[0] - 1, rest[1] - 1, place, 0)
-        else:
-            lax.fori_loop(0, LAYERS, place, 0)
+        for p in range(2):
+            for c in range(VARS):
+                rows = flat(q, p, c)
+                rows[column(FIRST - 1), :] = t_in[q, 0, p, c]
+                rows[column(LAST + 1), :] = t_in[q, 1, p, c]
 
     def axial_down(q):
         return remote(
@@ -348,9 +369,8 @@
             return src_edge[1, p, c]
         return src[p, c, l - 1, base - PAD : base - PAD + 8, :]
 
-    def tile_pair(q, l, first_row):
+    def tile_pair(q, l, bases):
         weight = 1.0 / (SECTIONS - q)
-        bases = [first_row, first_row + 8]
         acc = {}
 
         def add(key, value):
@@ -394,15 +414,25 @@
                     else:
                         v[q + 1, p, c, l, base : base + 8, :] = value
 
-    def stencil(q, first, last):
+    middle, sides = (PAD + 8, PAD + 16), (PAD, PAD + 24)
+
+    def stencil(q, first, last, *pairs):
         def layer(l, carry):
-            for half in range(2):
-                tile_pair(q, l, PAD + 16 * half)
+            for pair in pairs or (middle, sides):
+                tile_pair(q, l, pair)
             return carry
 
         lax.fori_loop(first, last, layer, 0)
 
-    def forward(q, group):
+    def outer_layers(q):
+        def layer(i, carry):
+            for pair in (middle, sides):
+                tile_pair(q, 1 + (LAYERS - 1) * i, pair)
+            return carry
+
+        lax.fori_loop(jnp.where(inlet, 1, 0), jnp.where(outlet, 1, 2), layer, 0)
+
+    def forward(q):
         blocks = []
         for c in range(VARS):
             blocks.append(
@@ -416,33 +446,53 @@
         rhs = jnp.concatenate([hi, lo, hi, jnp.zeros_like(hi)], axis=0)
         res = jnp.dot(wf[...], rhs, preferred_element_type=F32)
         for c in range(VARS):
-            parts[pl.ds(32 * (group + c), 32), :] = res[:, 128 * c : 128 * (c + 1)]
-
-    def send_parts(rd):
-        for u in range(3):
-            block = parts[pl.ds(128 * u, 128), :].T
-            sent[rd, :, :, 128 * u : 128 * (u + 1)] = block.reshape(nth, BAND, 128)
+            parts[pl.ds(32 * c, 32), :] = res[:, 128 * c : 128 * (c + 1)]
+
+    def pack_rows(q, at_):
+        total = jnp.zeros((32, 128), F32)
+        for i in range(4):
+            rows = spare[pl.ds(i, 32, stride=4), :]
+            shift = (32 * i - at_) % 128
+            rows = pltpu.roll(rows, shift, 1) if shift else rows
+            total = jnp.where(lanes(32) // 32 == i, rows, total)
+        for b in range(nth):
+            sent_x[q, b] = total[2 * b : 2 * b + 2]
+
+    def send_parts(q):
+        sent[q] = parts[pl.ds(0, 128), :].T.reshape(nth, BAND, 128)
+        spare[...] = parts[pl.ds(128, 128), :].T
+        pack_rows(q, 0)
+        if q == 0:
+            pack_rows(SECTIONS, 32)
 
         def one(i, carry):
             band = far_first(i)
             mine = on_my_side(band)
             own = jnp.logical_and(mine, band == t)
+            slot = jnp.where(mine, t, nth + t)
+            which = jnp.where(mine, 0, 1)
+            ways = [
+                (sent.at[q, band], got.at[q, slot], p_send.at[q], p_recv.at[q, which]),
+                (sent_x.at[q, band], got_x.at[q, slot], x_send.at[q], x_recv.at[q, which]),
+            ]
+            if q == 0:
+                ways.append(
+                    (
+                        sent_x.at[SECTIONS, band], got_dt.at[slot],
+                        x_send.at[SECTIONS], x_recv.at[SECTIONS, which],
+                    )
+                )
 
             @pl.when(own)
             def _():
-                pltpu.make_async_copy(
-                    sent.at[rd, band], got.at[rd, t], p_recv.at[rd, 0]
-                ).start()
+                for here, there, _, recv in ways:
+                    pltpu.make_async_copy(here, there, recv).start()
 
             @pl.when(jnp.logical_not(own))
             def _():
-                remote(
-                    sent.at[rd, band],
-                    got.at[rd, jnp.where(mine, t, nth + t)],
-                    p_send.at[rd],
-                    p_recv.at[rd, jnp.where(mine, 0, 1)],
-                    (jnp.where(mine, y, py), band, jnp.where(mine, a, pa)),
-                ).start()
+                device = (jnp.where(mine, y, py), band, jnp.where(mine, a, pa))
+                for here, there, send, recv in ways:
+                    remote(here, there, send, recv, device).start()
 
             return carry
 
@@ -492,94 +542,130 @@
             result.append(top + pltpu.roll(top, 96, 1) + low)
         return result
 
-    def serve(rd):
-        q = 2 * rd
-        wait_for(got.at[rd, pl.ds(0, nth)], p_recv.at[rd, 0])
-        pl.when(paired)(
-            lambda: wait_for(got.at[rd, pl.ds(nth, nth)], p_recv.at[rd, 1])
-        )
-        groups = []
+    sub8 = subs(8)
+
+    def unpacked(rows, at_=0):
+        wide = jnp.where(sub8 < 4, rows[0:1], rows[1:2])
+        result = wide
+        for i in range(4):
+            shift = (at_ - 32 * i) % 128
+            turned = pltpu.roll(wide, shift, 1) if shift else wide
+            result = jnp.where(lax.rem(sub8, 4) == i, turned, result)
+        return result
+
+    def packed(x):
+        total = jnp.zeros((8, 128), F32)
+        for i in range(4):
+            turned = pltpu.roll(x, 32 * i, 1) if i else x
+            total = jnp.where(lax.rem(sub8, 4) == i, turned, total)
+        return jnp.concatenate(
+            [
+                jnp.sum(total[0:4], axis=0, keepdims=True),
+                jnp.sum(total[4:8], axis=0, keepdims=True),
+            ],
+            axis=0,
+        )
+
+    def sums(q):
+        def arrive(which):
+            wait_for(got.at[q, pl.ds(which * nth, nth)], p_recv.at[q, which])
+            wait_for(got_x.at[q, pl.ds(which * nth, nth)], x_recv.at[q, which])
+            if q == 0:
+                wait_for(
+                    got_dt.at[pl.ds(which * nth, nth)], x_recv.at[SECTIONS, which]
+                )
+
+        arrive(0)
+        pl.when(paired)(lambda: arrive(1))
+        result = []
         for slot in range(2):
-            total = got[rd, slot * nth]
+            total, last = got[q, slot * nth], got_x[q, slot * nth]
             for i in range(1, nth):
-                total = total + got[rd, slot * nth + i]
-            pieces = []
-            for g in range(2 * VARS):
-                piece = total[:, 128 * (g // 4) : 128 * (g // 4 + 1)]
-                if g % 4:
-                    piece = pltpu.roll(piece, 128 - 32 * (g % 4), 1)
-                if slot == 1:
-                    piece = jnp.where(paired, piece, 0.0)
-                pieces.append(piece)
-            groups.append((pieces[:VARS], pieces[VARS:]))
-            if rd == 0:
-                for u in range(nth // 4):
-                    cells = jnp.zeros((8, 128), F32)
-                    for i in range(4):
-                        tile = got[rd, slot * nth + 4 * u + i, :, 256:384]
-                        if i != 2:
-                            tile = pltpu.roll(tile, (32 * i + 64) % 128, 1)
-                        cells = jnp.where(lane8 // 32 == i, tile, cells)
-                    dt_all[slot, :, 128 * u : 128 * (u + 1)] = cells
-        (own_now, own_next), (nbr_now, nbr_next) = groups
-        c_own = mixed(0, own_now, nbr_now)
-        c_nbr = mixed(1, nbr_now, own_now)
-        scale = 1.0 / (SECTIONS - q) / circle
-        own_next = [x - scale * r for x, r in zip(own_next, response(0, c_own))]
-        nbr_next = [
-            jnp.where(paired, x - scale * r, 0.0)
-            for x, r in zip(nbr_next, response(1, c_nbr))
-        ]
-        d_own = mixed(0, own_next, nbr_next)
-        d_nbr = mixed(1, nbr_next, own_next)
-        for slot, values in ((0, c_own + d_own), (1, c_nbr + d_nbr)):
-            for u in range(3):
-                total = jnp.zeros((8, 128), F32)
-                for i, x in enumerate(values[4 * u : 4 * u + 4]):
-                    total = total + (pltpu.roll(x, 32 * i, 1) if i else x)
-                c_out[rd, slot, :, 128 * u : 128 * (u + 1)] = total
+                total = total + got[q, slot * nth + i]
+                last = last + got_x[q, slot * nth + i]
+            pieces = [pltpu.roll(total, 128 - 32 * g, 1) if g else total for g in range(4)]
+            pieces.append(unpacked(last))
+            if slot == 1:
+                pieces = [jnp.where(paired, x, 0.0) for x in pieces]
+            result.append(pieces)
+        return result
+
+    def gather_steps():
+        for slot in range(2):
+            for u in range(nth // 4):
+                cells = jnp.zeros((8, 128), F32)
+                for i in range(4):
+                    tile = unpacked(got_dt[slot * nth + 4 * u + i], 32 * i)
+                    cells = jnp.where(lane8 // 32 == i, tile, cells)
+                dt_all[slot, :, 128 * u : 128 * (u + 1)] = cells
+
+    def send_modes(q, own, neighbour):
+        for slot, values in ((0, own), (1, neighbour)):
+            total = values[0]
+            for i in range(1, 4):
+                total = total + pltpu.roll(values[i], 32 * i, 1)
+            c_out[q, slot] = total
+            c_out_x[q, slot] = packed(values[4])
 
         def one(i, carry):
             theta = far_first(i)
 
-            @pl.when(paired)
-            def _():
+            def send(slot, device):
                 remote(
-                    c_out.at[rd, 1], c_in.at[rd, t], c_send.at[rd], c_recv.at[rd],
-                    (py, theta, pa),
+                    c_out.at[q, slot], c_in.at[q, t], c_send.at[q], c_recv.at[q], device
                 ).start()
-
-            @pl.when(theta != t)
-            def _():
                 remote(
-                    c_out.at[rd, 0], c_in.at[rd, t], c_send.at[rd], c_recv.at[rd],
-                    (y, theta, a),
+                    c_out_x.at[q, slot], c_in_x.at[q, t], y_send.at[q], y_recv.at[q], device
                 ).start()
+
+            pl.when(paired)(lambda: send(1, (py, theta, pa)))
+            pl.when(theta != t)(lambda: send(0, (y, theta, a)))
 
             @pl.when(theta == t)
             def _():
                 pltpu.make_async_copy(
-                    c_out.at[rd, 0], c_in.at[rd, t], c_recv.at[rd]
+                    c_out.at[q, 0], c_in.at[q, t], c_recv.at[q]
                 ).start()
+                pltpu.make_async_copy(
+                    c_out_x.at[q, 0], c_in_x.at[q, t], y_recv.at[q]
+                ).start()
 
             return carry
 
         lax.fori_loop(0, nth, one, 0)
 
-    def fixes(rd):
-        wait_for(c_in.at[rd], c_recv.at[rd])
-        rows = []
-        for u in range(3):
-            block = c_in[rd, :, :, 128 * u : 128 * (u + 1)].reshape(RADII, 128).T
-            rows.extend(block[32 * i : 32 * (i + 1)] for i in range(4))
-        result = []
-        for s in range(2):
-            x = jnp.concatenate(rows[VARS * s : VARS * (s + 1)], axis=1)
-            hi = x.astype(BF16)
-            lo = (x - hi.astype(F32)).astype(BF16)
-            rhs = jnp.concatenate([hi, lo, hi, jnp.zeros_like(hi)], axis=0)
-            result.append(jnp.dot(w2[...], rhs, preferred_element_type=F32))
-        return result
+    def serve(q):
+        own, nbr = sums(q)
+        c_own = mixed(0, own, nbr)
+        c_nbr = mixed(1, nbr, own)
+        send_modes(q, c_own, c_nbr)
+        if q == 0:
+            gather_steps()
+        scale = 1.0 / (SECTIONS - q) / circle
+        r_own, r_nbr = response(0, c_own), response(1, c_nbr)
+        own, nbr = sums(q + 1)
+        own = [x - scale * r for x, r in zip(own, r_own)]
+        nbr = [jnp.where(paired, x - scale * r, 0.0) for x, r in zip(nbr, r_nbr)]
+        send_modes(q + 1, mixed(0, own, nbr), mixed(1, nbr, own))
+
+    def fix_of(q):
+        wait_for(c_in.at[q], c_recv.at[q])
+        wait_for(c_in_x.at[q], y_recv.at[q])
+        block = c_in[q].reshape(RADII, 128).T
+        rows = [block[32 * i : 32 * (i + 1)] for i in range(4)]
+        for b in range(nth):
+            parts[pl.ds(2 * b, 2), :] = c_in_x[q, b]
+        last = parts[pl.ds(0, 32), :]
+        for i in range(4):
+            spare[pl.ds(i, 32, stride=4), :] = (
+                pltpu.roll(last, 128 - 32 * i, 1) if i else last
+            )
+        rows.append(spare[...].T[0:32])
+        x = jnp.concatenate(rows, axis=1)
+        hi = x.astype(BF16)
+        lo = (x - hi.astype(F32)).astype(BF16)
+        rhs = jnp.concatenate([hi, lo, hi, jnp.zeros_like(hi)], axis=0)
+        return jnp.dot(w2[...], rhs, preferred_element_type=F32)
 
     def subtract(q, fix, margin):
         weight = 1.0 / (SECTIONS - q)
@@ -620,6 +706,9 @@
             ]
         return copies
 
+    def plane_tile(i):
+        return v.at[0, :, :, edge, pl.ds((PAD + SECTOR, PAD - 8)[i], 8)]
+
     def tile_copies():
         return [
             remote(
@@ -650,8 +739,9 @@
 
     @pl.when(bnd)
     def _():
-        parts[pl.ds(320, 32), :] = dt[edge - 1, PAD : PAD + SECTOR, :]
-        forward(0, 0)
+        parts[pl.ds(160, 32), :] = dt[edge - 1, PAD : PAD + SECTOR, :]
+        forward(0)
+        send_parts(0)
 
     load_jac.wait()
 
@@ -667,66 +757,77 @@
     lax.fori_loop(0, LAYERS, spread, 0)
     load_source.wait()
 
-    far = (jnp.where(inlet, 3, 1), jnp.where(outlet, LAYERS - 1, LAYERS + 1))
+    far = (jnp.where(inlet, 3, 2), jnp.where(outlet, LAYERS - 1, LAYERS))
     near = jnp.where(inlet, 1, LAYERS - 1)
     second = jnp.where(inlet, 2, LAYERS - 1)
 
-    for rd in range(2):
-        q = 2 * rd
+    for q in (0, 2):
 
         @pl.when(bnd)
         def _():
-            if rd == 0:
-                for copy in edge_copies():
-                    copy.wait_recv()
-            for half in range(2):
-                tile_pair(q, edge, PAD + 16 * half)
-            if rd:
-                forward(q, 0)
-            forward(q + 1, VARS)
-            send_parts(rd)
-            if rd == 0:
+            if q == 0:
+                for i in range(2):
+                    wait_for(plane_tile(i), edge_recv.at[0, i])
+            else:
+                forward(q)
+                send_parts(q)
+            for pair in (middle, sides):
+                tile_pair(q, edge, pair)
+            forward(q + 1)
+            send_parts(q + 1)
+            if q == 0:
                 for copy in tile_copies():
                     copy.start()
 
+        if q:
+            send_theta(q)
+        stencil(q, 2, LAYERS, middle)
         take_theta(q)
-        take_axial(q)
-        stencil(q, *rest)
-        send_theta(q + 1)
-        send_axial(q + 1)
-
-        if rd == 0:
+        stencil(q, 2, LAYERS, sides)
+        if q == 0:
 
             @pl.when(served)
             def _():
                 pack_copy().wait_recv()
                 full_table(1)
 
-        pl.when(owner)(lambda: serve(rd))
+        take_axial(q)
+        outer_layers(q)
+        send_theta(q + 1)
+        send_axial(q + 1)
+        pl.when(owner)(lambda: serve(q))
+        stencil(q + 1, *far, middle)
+        if q == 0:
+
+            @pl.when(bnd)
+            def _():
+                for copy in tile_copies():
+                    copy.wait()
+
         take_theta(q + 1)
+        stencil(q + 1, *far, sides)
         take_axial(q + 1)
-        stencil(q + 1, *far)
-        if rd == 0:
+        outer_layers(q + 1)
+        if q == 0:
             send_axial(q + 2)
 
         @pl.when(bnd)
         def _():
-            now, later = fixes(rd)
-            if rd == 0:
-                for copy in tile_copies():
-                    copy.wait()
+            now = fix_of(q)
+            if q == 0:
+                for i in range(2):
+                    wait_for(dt.at[edge - 1, pl.ds(PAD, 8)], edge_recv.at[1, i])
+                    wait_for(src_edge.at[i], edge_recv.at[2, i])
                 subtract(q, now, 8)
                 for third in range(3):
-                    tile_pair(q + 1, edge, PAD - 8 + 16 * third)
+                    first = PAD - 8 + 16 * third
+                    tile_pair(q + 1, edge, (first, first + 8))
                 stencil(q + 1, second, second + 1)
-                subtract(q + 1, later, 8)
+                subtract(q + 1, fix_of(q + 1), 8)
             else:
                 subtract(q, now, 8)
                 stencil(q + 1, near, near + 2)
-                subtract(q + 1, later, 0)
-
-        if rd == 0:
-            send_theta(q + 2)
+                subtract(q + 1, fix_of(q + 1), 0)
 
     for q in range(SECTIONS):
         for copy in theta_copies(q):
@@ -739,17 +840,25 @@
         for copy in edge_copies():
             copy.wait_send()
         pl.when(helps)(lambda: pack_copy().wait_send())
-        for rd in range(2):
-            pl.when(owner)(
-                lambda: wait_for(sent.at[rd, pl.ds(0, nth - 1)], p_send.at[rd])
+        for q in range(SECTIONS):
+            alike = ((sent, p_send, got, c_send), (sent_x, x_send, got_x, y_send))
+            for mine, mine_sem, theirs, theirs_sem in alike:
+                pl.when(owner)(
+                    lambda: wait_for(mine.at[q, pl.ds(0, nth - 1)], mine_sem.at[q])
+                )
+                pl.when(helps)(lambda: wait_for(mine.at[q], mine_sem.at[q]))
+                pl.when(served)(
+                    lambda: wait_for(theirs.at[q, pl.ds(0, 2 * nth - 1)], theirs_sem.at[q])
+                )
+                pl.when(jnp.logical_and(owner, alone))(
+                    lambda: wait_for(theirs.at[q, pl.ds(0, nth - 1)], theirs_sem.at[q])
+                )
+        pl.when(owner)(
+            lambda: wait_for(
+                sent_x.at[SECTIONS, pl.ds(0, nth - 1)], x_send.at[SECTIONS]
             )
-            pl.when(helps)(lambda: wait_for(sent.at[rd], p_send.at[rd]))
-            pl.when(served)(
-                lambda: wait_for(got.at[rd, pl.ds(0, 2 * nth - 1)], c_send.at[rd])
-            )
-            pl.when(jnp.logical_and(owner, alone))(
-                lambda: wait_for(got.at[rd, pl.ds(0, nth - 1)], c_send.at[rd])
-            )
+        )
+        pl.when(helps)(lambda: wait_for(sent_x.at[SECTIONS], x_send.at[SECTIONS]))
 
 
 def solution(mesh):
@@ -766,9 +875,12 @@
         return pl.pallas_call(
             functools.partial(kernel, (nrow, nth, nax, circle)),
             out_shape=pltpu.VMEM(state.shape, F32),
-            in_specs=[anyspace] * 4 + [scalars] * 4,
+            in_specs=[anyspace] * 7 + [scalars],
             out_specs=pl.BlockSpec(memory_space=pltpu.VMEM),
             scratch_shapes=[
+                pltpu.SMEM(order.shape, jnp.int32),
+                pltpu.SMEM(giles.shape, F32),
+                pltpu.SMEM(coupling.shape, F32),
                 pltpu.VMEM((SECTIONS, *cells, LAYERS + 2, 2 * PAD + SECTOR, RADII), F32),
                 pltpu.VMEM((*cells, LAYERS, SECTOR, RADII), F32),
                 pltpu.VMEM((2, *cells, 8, RADII), F32),
@@ -781,13 +893,19 @@
                 pltpu.VMEM((2 * (SECTOR + 16), 128), BF16),
                 pltpu.VMEM((2, 128, 2 * circle), BF16),
                 pltpu.VMEM((2, 104, 128), F32),
-                pltpu.VMEM((WIDE, 128), F32),
-                pltpu.VMEM((2, nth, BAND, WIDE), F32),
-                pltpu.VMEM((2, 2 * nth, BAND, WIDE), F32),
+                pltpu.VMEM((256, 128), F32),
+                pltpu.VMEM((SECTIONS, nth, BAND, 128), F32),
+                pltpu.VMEM((SECTIONS + 1, nth, 2, 128), F32),
+                pltpu.VMEM((SECTIONS, 2 * nth, BAND, 128), F32),
+                pltpu.VMEM((SECTIONS, 2 * nth, 2, 128), F32),
+                pltpu.VMEM((2 * nth, 2, 128), F32),
                 pltpu.VMEM((2, BAND, circle), F32),
-                pltpu.VMEM((2, 2, BAND, WIDE), F32),
-                pltpu.VMEM((2, nth, BAND, WIDE), F32),
-                dma((4,)),
+                pltpu.VMEM((SECTIONS, 2, BAND, 128), F32),
+                pltpu.VMEM((SECTIONS, 2, 2, 128), F32),
+                pltpu.VMEM((SECTIONS, nth, BAND, 128), F32),
+                pltpu.VMEM((SECTIONS, nth, 2, 128), F32),
+                pltpu.VMEM((RADII, 128), F32),
+                dma((7,)),
                 dma((SECTIONS, 2)),
                 dma((SECTIONS, 2)),
                 dma((SECTIONS, 2)),
@@ -797,10 +915,14 @@
                 dma((2,)),
                 dma((2,)),
                 dma((2,)),
-                dma((2,)),
-                dma((2, 2)),
-                dma((2,)),
-                dma((2,)),
+                dma((SECTIONS,)),
+                dma((SECTIONS, 2)),
+                dma((SECTIONS + 1,)),
+                dma((SECTIONS + 1, 2)),
+                dma((SECTIONS,)),
+                dma((SECTIONS,)),
+                dma((SECTIONS,)),
+                dma((SECTIONS,)),
             ],
             compiler_params=pltpu.CompilerParams(
                 collective_id=0, has_side_effects=True, vmem_limit_bytes=VMEM_LIMIT

time: 51.5 us -> 47.6 us (0.924)
  Pallas kernels: 49.6 us -> 45.7 us
    pallas_call x1, Pallas kernels: 49.6 us -> 45.7 us  [step(): pl.pallas_call(functools.partial(kernel, (nrow, nth, nax, circle)), out_s...]
where the time goes in v2:
time: 47.6 us; the launch traced here: 47.5 us
  Pallas kernels  45.7 us (96%)
  local copies, waits for them, and re-layouts  1.06 us (2%)
  between operations  0.66 us (1%)
    pallas_call x1, Pallas kernels, step(): pl.pallas_call(functools.partial(kernel, (nrow, nth, nax, circle)), out_s...  45.7 us
    unnamed x1, local copies, waits for them, and re-layouts  1.06 us

profile of v2, /device:TPU:7, one launch (start us, length us, event | category | flops | bytes accessed | tf_op | source)
XLA Modules:
  0.0 47.5 jit_solution(9585147262626403697)
XLA Ops:
  0.7 45.7 %shard_map.82 = f32[1,2,5,8,32,128]{5,4,3,2,1,0:T(8,128)S(1)} custom-call(f32[1,2,5,8,32,128]{5,4,3,2,1,0:T(8,128)} %state_in.1, f32[1,2,5,8,32,128]{5,4,3,2,1,0:T(8,128)} %source_in.1, f32[1,8,32,128]{3,2,1,0:T(8,128)} %step_in.1, f32[1,3,5,5,8,128]{5,4,3,2,1,0:T(8,128)} %jac_in.1, s32[1,512]{1,0:T(1,128)} %order_in.1, f32[1,2,2,5,2,5]{5,4,3,2,1,0:T(2,128)} %bitcast.2, ...), custom_call_target="tpu_custom_call" | custom-call | tf_op jit(solution)/shard_map/pallas_call | solution.py:875
  46.4 1.1 %copy.10 = f32[1,2,5,8,32,128]{5,4,3,2,1,0:T(8,128)} copy(f32[1,2,5,8,32,128]{5,4,3,2,1,0:T(8,128)S(1)} %shard_map.82) | data formatting | bytes 2621440

commit v3 on v2

--- a/solution.py
+++ b/solution.py
@@ -281,18 +281,6 @@
                 (2, VARS, 2 * PAD + SECTOR, 128), F32
             )
 
-    pl.semaphore_wait(
-        barrier,
-        2
-        + jnp.where(a > 0, 1, 0)
-        + jnp.where(a < nax - 1, 1, 0)
-        + jnp.where(
-            bnd,
-            jnp.where(owner, jnp.where(paired, 2 * nth - 1, nth - 1), nth),
-            0,
-        ),
-    )
-
     def remote(src_ref, dst_ref, send, recv, device):
         return pltpu.make_async_remote_copy(
             src_ref=src_ref,
@@ -318,12 +306,15 @@
     def column(row):
         return pl.ds(2 * PAD + SECTOR + row, LAYERS, stride=2 * PAD + SECTOR)
 
-    def send_theta(q):
+    def stage_theta(q):
         for p in range(2):
             for c in range(VARS):
                 rows = flat(q, p, c)
                 t_out[q, 0, p, c] = rows[column(FIRST), :]
                 t_out[q, 1, p, c] = rows[column(LAST), :]
+
+    def send_theta(q):
+        stage_theta(q)
         for copy in theta_copies(q):
             copy.start()
 
@@ -458,13 +449,14 @@
         for b in range(nth):
             sent_x[q, b] = total[2 * b : 2 * b + 2]
 
-    def send_parts(q):
+    def stage_parts(q):
         sent[q] = parts[pl.ds(0, 128), :].T.reshape(nth, BAND, 128)
         spare[...] = parts[pl.ds(128, 128), :].T
         pack_rows(q, 0)
         if q == 0:
             pack_rows(SECTIONS, 32)
 
+    def send_parts(q):
         def one(i, carry):
             band = far_first(i)
             mine = on_my_side(band)
@@ -496,7 +488,7 @@
 
             return carry
 
-        lax.fori_loop(0, nth, one, 0)
+        lax.fori_loop(0, nth, one, 0, unroll=4)
 
     def swapped(x):
         return jnp.where(lane8 < MODES, pltpu.roll(x, 128 - MODES, 1), pltpu.roll(x, MODES, 1))
@@ -632,7 +624,7 @@
 
             return carry
 
-        lax.fori_loop(0, nth, one, 0)
+        lax.fori_loop(0, nth, one, 0, unroll=4)
 
     def serve(q):
         own, nbr = sums(q)
@@ -692,7 +684,7 @@
             rows, place, device = pl.ds(at_, 8), pl.ds(row, 8), (y, device, a)
             copies += [
                 remote(
-                    state_in.at[0, :, :, plane, rows], v.at[0, :, :, edge, place],
+                    v.at[0, :, :, edge, pl.ds(PAD + at_, 8)], v.at[0, :, :, edge, place],
                     edge_send.at[0, i], edge_recv.at[0, i], device,
                 ),
                 remote(
@@ -726,23 +718,6 @@
     helps = jnp.logical_and(bnd, jnp.logical_not(owner))
     served = jnp.logical_and(owner, paired)
 
-    @pl.when(bnd)
-    def _():
-        for copy in edge_copies():
-            copy.start()
-        pl.when(helps)(lambda: pack_copy().start())
-
-    load_state.wait()
-    send_theta(0)
-    send_axial(0)
-    load_step.wait()
-
-    @pl.when(bnd)
-    def _():
-        parts[pl.ds(160, 32), :] = dt[edge - 1, PAD : PAD + SECTOR, :]
-        forward(0)
-        send_parts(0)
-
     load_jac.wait()
 
     def spread(l, carry):
@@ -755,6 +730,43 @@
         return carry
 
     lax.fori_loop(0, LAYERS, spread, 0)
+    load_state.wait()
+    load_step.wait()
+
+    @pl.when(bnd)
+    def _():
+        parts[pl.ds(160, 32), :] = dt[edge - 1, PAD : PAD + SECTOR, :]
+        forward(0)
+        stage_parts(0)
+
+    stage_theta(0)
+
+    pl.semaphore_wait(
+        barrier,
+        2
+        + jnp.where(a > 0, 1, 0)
+        + jnp.where(a < nax - 1, 1, 0)
+        + jnp.where(
+            bnd,
+            jnp.where(owner, jnp.where(paired, 2 * nth - 1, nth - 1), nth),
+            0,
+        ),
+    )
+
+
+    @pl.when(bnd)
+    def _():
+        copies = edge_copies()
+        for copy in copies[::3]:
+            copy.start()
+        send_parts(0)
+        for i in (1, 4, 2, 5):
+            copies[i].start()
+        pl.when(helps)(lambda: pack_copy().start())
+
+    for copy in theta_copies(0):
+        copy.start()
+    send_axial(0)
     load_source.wait()
 
     far = (jnp.where(inlet, 3, 2), jnp.where(outlet, LAYERS - 1, LAYERS))
@@ -770,10 +782,12 @@
                     wait_for(plane_tile(i), edge_recv.at[0, i])
             else:
                 forward(q)
+                stage_parts(q)
                 send_parts(q)
             for pair in (middle, sides):
                 tile_pair(q, edge, pair)
             forward(q + 1)
+            stage_parts(q + 1)
             send_parts(q + 1)
             if q == 0:
                 for copy in tile_copies():

time: 47.6 us -> 45.7 us (0.960)
  Pallas kernels: 45.7 us -> 43.9 us
    pallas_call x1, Pallas kernels: 45.7 us -> 43.9 us  [step(): pl.pallas_call(functools.partial(kernel, (nrow, nth, nax, circle)), out_s...]
where the time goes in v3:
time: 45.7 us; the launch traced here: 45.6 us
  Pallas kernels  43.9 us (96%)
  local copies, waits for them, and re-layouts  1.06 us (2%)
  between operations  0.66 us (1%)
    pallas_call x1, Pallas kernels, step(): pl.pallas_call(functools.partial(kernel, (nrow, nth, nax, circle)), out_s...  43.9 us
    unnamed x1, local copies, waits for them, and re-layouts  1.06 us

profile of v3, /device:TPU:7, one launch (start us, length us, event | category | flops | bytes accessed | tf_op | source)
XLA Modules:
  0.0 45.6 jit_solution(337491353330598564)
XLA Ops:
  0.7 43.9 %shard_map.82 = f32[1,2,5,8,32,128]{5,4,3,2,1,0:T(8,128)S(1)} custom-call(f32[1,2,5,8,32,128]{5,4,3,2,1,0:T(8,128)} %state_in.1, f32[1,2,5,8,32,128]{5,4,3,2,1,0:T(8,128)} %source_in.1, f32[1,8,32,128]{3,2,1,0:T(8,128)} %step_in.1, f32[1,3,5,5,8,128]{5,4,3,2,1,0:T(8,128)} %jac_in.1, s32[1,512]{1,0:T(1,128)} %order_in.1, f32[1,2,2,5,2,5]{5,4,3,2,1,0:T(2,128)} %bitcast.2, ...), custom_call_target="tpu_custom_call" | custom-call | tf_op jit(solution)/shard_map/pallas_call | solution.py:889
  44.6 1.1 %copy.10 = f32[1,2,5,8,32,128]{5,4,3,2,1,0:T(8,128)} copy(f32[1,2,5,8,32,128]{5,4,3,2,1,0:T(8,128)S(1)} %shard_map.82) | data formatting | bytes 2621440

commit v4 on v3

--- a/solution.py
+++ b/solution.py
@@ -766,7 +766,8 @@
 
     for copy in theta_copies(0):
         copy.start()
-    send_axial(0)
+    pl.when(jnp.logical_or(a == 1, a == nax - 1))(lambda: axial_down(0).start())
+    pl.when(jnp.logical_or(a == 0, a == nax - 2))(lambda: axial_up(0).start())
     load_source.wait()
 
     far = (jnp.where(inlet, 3, 2), jnp.where(outlet, LAYERS - 1, LAYERS))
@@ -796,6 +797,9 @@
         if q:
             send_theta(q)
         stencil(q, 2, LAYERS, middle)
+        if q == 0:
+            pl.when(jnp.logical_and(a > 1, a < nax - 1))(lambda: axial_down(0).start())
+            pl.when(jnp.logical_and(a > 0, a < nax - 2))(lambda: axial_up(0).start())
         take_theta(q)
         stencil(q, 2, LAYERS, sides)
         if q == 0:

time: 45.7 us -> 46.4 us (1.015)
  Pallas kernels: 43.9 us -> 44.5 us
    pallas_call x1, Pallas kernels: 43.9 us -> 44.5 us  [step(): pl.pallas_call(functools.partial(kernel, (nrow, nth, nax, circle)), out_s...]
where the time goes in v4:
time: 46.4 us; the launch traced here: 46.3 us
  Pallas kernels  44.5 us (96%)
  local copies, waits for them, and re-layouts  1.06 us (2%)
  between operations  0.66 us (1%)
    pallas_call x1, Pallas kernels, step(): pl.pallas_call(functools.partial(kernel, (nrow, nth, nax, circle)), out_s...  44.5 us
    unnamed x1, local copies, waits for them, and re-layouts  1.06 us

profile of v4, /device:TPU:7, one launch (start us, length us, event | category | flops | bytes accessed | tf_op | source)
XLA Modules:
  0.0 46.3 jit_solution(3908402860788302331)
XLA Ops:
  0.7 44.5 %shard_map.82 = f32[1,2,5,8,32,128]{5,4,3,2,1,0:T(8,128)S(1)} custom-call(f32[1,2,5,8,32,128]{5,4,3,2,1,0:T(8,128)} %state_in.1, f32[1,2,5,8,32,128]{5,4,3,2,1,0:T(8,128)} %source_in.1, f32[1,8,32,128]{3,2,1,0:T(8,128)} %step_in.1, f32[1,3,5,5,8,128]{5,4,3,2,1,0:T(8,128)} %jac_in.1, s32[1,512]{1,0:T(1,128)} %order_in.1, f32[1,2,2,5,2,5]{5,4,3,2,1,0:T(2,128)} %bitcast.2, ...), custom_call_target="tpu_custom_call" | custom-call | tf_op jit(solution)/shard_map/pallas_call | solution.py:893
  45.2 1.1 %copy.10 = f32[1,2,5,8,32,128]{5,4,3,2,1,0:T(8,128)} copy(f32[1,2,5,8,32,128]{5,4,3,2,1,0:T(8,128)S(1)} %shard_map.82) | data formatting | bytes 2621440
